TPU v7x, 128 devices: a whole 4x4x4 slice. The times are simulated.
128 devices in a mesh: glob: 8 (over x, y_lo), reg: 16 (over z, y_hi, core).
Axes of the slice: x: 4, y: 4 (y_hi: 2, y_lo: 2; y = y_hi * 2 + y_lo), z: 4, core: 2. Of those that a mesh axis runs over, the one named last changes fastest.
Arguments:
- global_state: bfloat16 [128, 1024, 512], P('glob', 'reg'), may hold values from -6 to 6
- norm_gain: float32 [512], replicated, may hold values from 0.1 to 1.9
- qkv_weight: bfloat16 [512, 1536], replicated, may hold values from -0.25 to 0.25
- out_weight: bfloat16 [512, 512], replicated, may hold values from -0.25 to 0.25
- position_bias: float32 [8, 128, 128], replicated, may hold values from -4 to 262
- regional_state: bfloat16 [99, 128, 2048], P(None, 'glob', 'reg'), may hold values from -6 to 6
- conv_state: bfloat16 [9, 256, 99], replicated, may hold values from -0.1875 to 0.1875
- cond_weight: bfloat16 [256, 512], replicated, may hold values from -0.25 to 0.25
- conv_mid: bfloat16 [9, 256, 256], replicated, may hold values from -0.125 to 0.125
- conv_out: bfloat16 [9, 99, 256], replicated, may hold values from -0.125 to 0.125
- blocks: bfloat16 [64, 2048], replicated, may hold values from 0 to 0.25
- sources: int32 [8, 16, 64], P('glob', 'reg'), may hold values from 0 to 131071, as said below
- block_ids: int32 [8, 16, 64], P('glob', 'reg'), may hold values from 0 to 63, each once within a row
- shift_offset: int32 [1], replicated, may hold values from 1 to 7
Outputs:
- global_next: bfloat16 [128, 1024, 512], P('glob', 'reg')
- regional_next: float32 [99, 128, 2048], P(None, 'glob', 'reg')
Inputs may be any that keep to these rules, and one draw needn't show every extreme that they name: sources[i, j, :] belongs to the tile in tile row i, tile column j and gives global tokens as row * 1024 + column; it names only tokens of latitude band i (global rows i * 16 to i * 16 + 15); all tiles name only tokens of two neighbouring longitude sectors, global columns s * 64 to s * 64 + 2 * 64 - 1 for one s, and every tile names some token of each of these two sectors. `block_ids`: each tile names every block once.
All inputs are finite; a program needn't handle non-finite values.
Results may differ from a plain program's by a relative error of at most 0.006.
Values may be sent and summed in bfloat16 or wider, within the bound.
A program may use at most 128 MiB of HBM per device.

v0:
```python
import jax
import jax.numpy as jnp
from jax import lax
from jax.experimental import pallas as pl
from jax.experimental.pallas import tpu as pltpu
from jax.sharding import PartitionSpec as P

MESH = pl.DeviceIdType.MESH
F32 = jnp.float32
BF16 = jnp.bfloat16
NG, NR = 8, 16
PITCH, LEAD = 144, 8
NT = (((1,), (1,)), ((), ()))


def dot(a, b):
    return jnp.dot(a, b, preferred_element_type=F32)


def dot_nt(a, b):
    return lax.dot_general(a, b, NT, preferred_element_type=F32)


def silu(u):
    half = 0.5 * u
    return half + half * jnp.tanh(half)


def rows_at(index, count):
    return pl.ds(pl.multiple_of(index, 16), count)


def body(
    shift_ref, src_ref, bid_ref, gain_ref,
    gs_hbm, rs_hbm, qkvw_hbm, outw_hbm, bias_hbm, cs_hbm, cw_hbm, cm_hbm, co_hbm, blk_hbm,
    gnext_hbm, rnext_hbm,
    own, rsv, qkvw, outw, bias, csv, cw, cmv, cov, blk,
    sb, pb, fb, slab, sg, xs, xn, qkv, mixed, span, onext, yv, sel, zs, zr, z2, zc,
    st32, edge, el, er, rl, rr, xf, x3, hu, hd, p1, w1, w2, w3, amat, xm, x2, ost,
    lsem, psend, precv, fsend, frecv, esend, erecv, hsend, hrecv, gsend, grecv,
    asend, arecv, bsend, brecv, nsend, nrecv, osem,
):
    g = lax.axis_index("glob")
    r = lax.axis_index("reg")
    odd = lax.rem(g, 2)
    core = lax.rem(r, 2)
    chip = r // 2
    shift = shift_ref[0]
    partner = (g + 1 - 2 * odd, r)
    ahead = (lax.rem(g + 2 - 4 * odd + NG, NG), r)
    behind = (lax.rem(g - 2 + 4 * odd + NG, NG), r)
    other = (lax.rem(g - 1 + 2 * odd + NG, NG), r)
    mate = (g, r + 1 - 2 * core)
    far = (g, lax.rem(r - 1 + 2 * core + NR, NR))
    up, down = (lax.rem(g + NG - 1, NG), r), (lax.rem(g + 1, NG), r)
    left, right = (g, lax.rem(r + NR - 1, NR)), (g, lax.rem(r + 1, NR))
    chips = [(g, lax.rem(r + 2 * d, NR)) for d in range(1, 8)]
    around = [
        (a, b, (lax.rem(g + a + NG, NG), lax.rem(r + b + NR, NR)))
        for a in (-1, 0, 1) for b in (-1, 0, 1) if (a, b) != (0, 0)
    ]

    bar = pltpu.get_barrier_semaphore()
    greet = [partner, other, behind, mate, far] + chips + [t for a, b, t in around if a and b]
    for target in greet:
        pl.semaphore_signal(bar, inc=1, device_id=target, device_id_type=MESH)
    local = [
        (gs_hbm, own), (rs_hbm, rsv), (qkvw_hbm, qkvw), (bias_hbm, bias), (outw_hbm, outw),
        (blk_hbm, blk), (cs_hbm, csv), (cw_hbm, cw), (cm_hbm, cmv), (co_hbm, cov),
    ]
    loads = [pltpu.make_async_copy(a, b, lsem.at[i]) for i, (a, b) in enumerate(local)]
    for copy in loads:
        copy.start()

    def remote(src, dst, ssem, rsem, target):
        return pltpu.make_async_remote_copy(
            src_ref=src, dst_ref=dst, send_sem=ssem, recv_sem=rsem,
            device_id=target, device_id_type=MESH,
        )

    loads[0].wait()
    for i in range(8):
        sb[i] = own[i + jnp.where(i < 8 - shift, 0, 8)]
    slab[...] = jnp.zeros(slab.shape, jnp.int32)
    slab[0:1, 0:64] = src_ref[...]
    sg[chip, core] = slab[...]
    zc[:, 192:256, :] = jnp.zeros((3, 64, 256), BF16)
    pl.semaphore_wait(bar, len(greet))

    def halo_copy(c):
        start = 2 * c + odd * (6 - 4 * c)
        return remote(sb.at[pl.ds(start, 2)], pb.at[pl.ds(start, 2)], psend.at[c], precv.at[c], partner)

    def halo_in(c):
        start = 6 - 2 * c + odd * (4 * c - 6)
        return remote(sb.at[pl.ds(start, 2)], pb.at[pl.ds(start, 2)], psend.at[c], precv.at[c], partner)

    def forward_copy(c):
        if c == 3:
            at = pl.ds(1 + 5 * odd, 1)
        else:
            at = pl.ds(6 - 2 * c + odd * (4 * c - 6), 2)
        return remote(pb.at[at], fb.at[at], fsend.at[c], frecv.at[c], ahead)

    sends = [halo_copy(c) for c in range(4)]
    for copy in sends:
        copy.start()
    mate_slab = remote(slab, sg.at[chip, core], gsend.at[0], grecv.at[0], mate)
    mate_slab.start()
    sends.append(mate_slab)
    forwards = [forward_copy(c) for c in range(4)]

    def forward(c):
        halo_in(c).wait_recv()
        forwards[c].start()

    loads[1].wait()
    st32[0:1584, :] = rsv[...].reshape(1584, 128).astype(F32)
    st32[1584:2048, :] = jnp.zeros((464, 128), F32)

    def turn(y, _):
        cells = st32[pl.ds(y, 128, stride=16), :].T
        xf[pl.ds(pl.multiple_of(y * PITCH + LEAD, 8), 128), :] = cells
        at = pl.ds(pl.multiple_of(y * 8, 8), 8)
        edge[0, at, :] = cells[0:8]
        edge[1, at, :] = cells[120:128]
        return 0

    lax.fori_loop(0, 16, turn, 0)
    el[...] = edge[0].astype(BF16)
    er[...] = edge[1].astype(BF16)
    edges = [
        remote(el, rr, esend.at[0], erecv.at[0], left),
        remote(er, rl, esend.at[1], erecv.at[1], right),
    ]
    for copy in edges:
        copy.start()
    sends += edges

    mate_slab.wait_recv()
    slabs = [
        remote(sg.at[chip], sg.at[chip], gsend.at[1 + i], grecv.at[1 + i], t) for i, t in enumerate(chips)
    ]
    for copy in slabs:
        copy.start()
    sends += slabs
    forward(0)

    lanes = lax.broadcasted_iota(jnp.int32, (128, 128), 1)
    low = lanes < 64
    key_row = lax.broadcasted_iota(jnp.int32, (1, 128), 1) // 16

    def place(j, row):
        for w in range(4):
            xs[w * 128 + j * 16 : w * 128 + j * 16 + 16, :] = row[w * 16 : w * 16 + 16, :]

    def attend(k):
        def norm(w, _):
            at = pl.ds(pl.multiple_of(w * 128, 128), 128)
            values = xs[at, :].astype(F32)
            center = values - jnp.mean(values, axis=-1, keepdims=True)
            spread = jnp.mean(center * center, axis=-1, keepdims=True)
            xn[at, :] = (center * lax.rsqrt(spread + 1e-05) * gain_ref[...]).astype(BF16)
            return 0

        lax.fori_loop(0, 4, norm, 0)
        qkv[:, 0:512] = (dot(xn[...], qkvw[:, 0:512]).astype(BF16) * 0.125).astype(BF16)
        qkv[:, 512:1024] = dot(xn[...], qkvw[:, 512:1024]).astype(BF16)
        qkv[:, 1024:1536] = dot(xn[...], qkvw[:, 1024:1536]).astype(BF16)
        row_id = 16 * g - shift + 8 * k + key_row
        absent = jnp.where((row_id >= 0) & (row_id < 16 * NG), 0.0, -jnp.inf).astype(F32)
        ones = jnp.ones((128, 128), BF16)

        def window(w, _):
            at = pl.ds(pl.multiple_of(w * 128, 128), 128)
            for hp in range(4):
                q = qkv[at, hp * 128 : hp * 128 + 128]
                key = qkv[at, 512 + hp * 128 : 512 + hp * 128 + 128]
                val = qkv[at, 1024 + hp * 128 : 1024 + hp * 128 + 128]
                zero = jnp.zeros_like(q)
                q2 = jnp.concatenate([jnp.where(low, q, zero), jnp.where(low, zero, q)], axis=0)
                scores = dot_nt(q2, key) + bias[2 * hp : 2 * hp + 2].reshape(256, 128) + absent
                peak = jnp.max(scores, axis=-1, keepdims=True)
                weight = jnp.exp(scores - peak).astype(BF16)
                both = dot(weight, jnp.concatenate([val, ones], axis=1))
                out = both[:, 0:128] / both[:, 128:256]
                mixed[at, hp * 128 : hp * 128 + 128] = jnp.where(low, out[0:128], out[128:256]).astype(BF16)
            return 0

        lax.fori_loop(0, 4, window, 0)
        update = dot(mixed[...], outw[...])
        result = (xs[...].astype(F32) + update).astype(BF16)
        for w in range(4):
            for j in range(8):
                span[8 * k + j, w * 16 : w * 16 + 16, :] = result[w * 128 + j * 16 : w * 128 + j * 16 + 16]

    loads[2].wait()
    loads[3].wait()
    loads[4].wait()
    for j in range(8):
        place(j, own[8 - shift + j])
    attend(1)
    forward(1)

    for i in range(5, 10):
        loads[i].wait()
    for o in range(9):
        w1[:, o * 128 : o * 128 + 128] = jnp.concatenate([csv[o], jnp.zeros((256, 29), BF16)], axis=1)
        w2[:, o * 256 : o * 256 + 256] = cmv[o]
        a, b = o // 3, o % 3
        w3[b * 128 : b * 128 + 128, a * 256 : a * 256 + 256] = jnp.concatenate(
            [cov[o].astype(F32), jnp.zeros((29, 256), F32)], axis=0
        ).astype(BF16)

    def interpolation(y, _):
        part = blk[:, pl.ds(pl.multiple_of(y * 128, 128), 128)].astype(F32)
        cells = jnp.concatenate([part, jnp.zeros((64, 128), F32)], axis=0).T
        main = jnp.concatenate(
            [pltpu.roll(cells[120:128], 64, 1), cells, jnp.zeros((8, 128), F32)], axis=0
        )
        side = jnp.concatenate([jnp.zeros((136, 128), F32), cells[0:8]], axis=0)
        amat[rows_at(y * PITCH, PITCH), :] = jnp.concatenate([main, side], axis=1).astype(BF16)
        return 0

    lax.fori_loop(0, 16, interpolation, 0)
    forward(2)

    for copy in edges:
        copy.wait_recv()
    edge[0] = jnp.where(r > 0, rl[...].astype(F32), 0.0)
    edge[1] = jnp.where(r < NR - 1, rr[...].astype(F32), 0.0)

    def spread3(cells):
        width = cells.shape[0]
        return jnp.concatenate([pltpu.roll(cells, 1, 0), cells, pltpu.roll(cells, width - 1, 0)], axis=1).astype(BF16)

    def frame(y, _):
        at = pl.ds(pl.multiple_of(y * 8, 8), 8)
        main = xf[pl.ds(pl.multiple_of(y * PITCH + LEAD, 8), 128), :]
        cells = jnp.concatenate([edge[0, at, :], main, edge[1, at, :]], axis=0)
        x3[rows_at((y + 3) * PITCH, PITCH), :] = spread3(cells)
        return 0

    lax.fori_loop(0, 16, frame, 0)
    borders = [
        remote(x3.at[pl.ds(3 * PITCH, 3 * PITCH), pl.ds(128, 128)], hd, hsend.at[0], hrecv.at[0], up),
        remote(x3.at[pl.ds(16 * PITCH, 3 * PITCH), pl.ds(128, 128)], hu, hsend.at[1], hrecv.at[1], down),
    ]
    for copy in borders:
        copy.start()
    sends += borders
    forward(3)

    def first_conv(y0, count):
        parts = [x3[rows_at((y0 + a) * PITCH, count * PITCH), :] for a in range(3)]
        p1[rows_at(y0 * PITCH, count * PITCH), :] = dot_nt(jnp.concatenate(parts, axis=1), w1[...])

    lax.fori_loop(0, 2, lambda i, _: (first_conv(3 + 7 * i, 7), 0)[1], 0)

    for copy in slabs:
        copy.wait_recv()
    ids = sg[...].reshape(128, 128)[0:128]
    ids = jnp.concatenate([ids[8 * j : 8 * j + 1] for j in range(16)], axis=0)
    row = lax.shift_right_logical(ids, 10) - 16 * g
    col = jnp.bitwise_and(ids, 1023) - 64 * r
    token = jnp.where((col >= 0) & (col < 64), row * 64 + col, -1).astype(F32)
    token = jnp.concatenate([token, jnp.zeros((112, 128), F32)], axis=0).T
    position = lax.broadcasted_iota(jnp.int32, (64, 1024), 1).astype(F32)
    for j in range(16):
        hit = token[0:64, j : j + 1] == position
        sel[j % 2, (j // 2) * 64 : (j // 2) * 64 + 64, :] = jnp.where(hit, 1.0, 0.0).astype(BF16)
    slots = lax.broadcasted_iota(jnp.int32, (64, 64), 0)
    perm = jnp.where(slots == bid_ref[...], 1.0, 0.0).astype(BF16)

    def cross(k, halo):
        below = k // 2
        for j in range(8):
            mine = below * (16 - shift + j) + (1 - below) * (j - shift)
            theirs = below * (j - shift) + (1 - below) * (8 - shift + j)
            inside = jnp.where(below == 1, j < shift, j >= shift)
            a = own[jnp.clip(mine, 0, 15)]
            b = halo[jnp.clip(theirs, 0, 7)]
            place(j, jnp.where(inside, a, b))
        attend(k)

    cross(2 - 2 * odd, pb)
    for copy in forwards:
        copy.wait_recv()
    cross(2 * odd, fb)

    for i in range(16):
        onext[i] = span[shift + i]
    store_g = pltpu.make_async_copy(onext, gnext_hbm, osem.at[0])
    store_g.start()
    yv[...] = dot_nt(onext[...].reshape(1024, 512), cw[...]).astype(BF16)
    zs[1 - core] = dot(sel[1 - core], yv[...]).astype(BF16)
    to_mate = remote(zs.at[1 - core], zr, asend, arecv, mate)
    to_mate.start()
    zs[core] = dot(sel[core], yv[...]).astype(BF16)
    to_mate.wait()
    zs[core] = zs[core] + zr[...]
    tiles = []
    for i, t in enumerate(chips):
        q = lax.rem(chip + i + 1, 8)
        tiles.append(remote(zs.at[core, rows_at(q * 64, 64)], z2.at[i], bsend.at[i], brecv.at[i], t))
    for copy in tiles:
        copy.start()
    for copy in borders:
        copy.wait_recv()
    for a in range(3):
        at = pl.ds(a * PITCH, PITCH)
        x3[a * PITCH : (a + 1) * PITCH, :] = spread3(jnp.where(g > 0, hu[at, :].astype(F32), 0.0))
        x3[(19 + a) * PITCH : (20 + a) * PITCH, :] = spread3(jnp.where(g < NG - 1, hd[at, :].astype(F32), 0.0))
    lax.fori_loop(0, 2, lambda i, _: (first_conv(17 * i, 3), 0)[1], 0)
    total = zs[core, rows_at(chip * 64, 64), :].astype(F32)
    for copy in tiles:
        copy.wait()
    for i in range(7):
        total = total + z2[i].astype(F32)
    zc[1, 0:64, :] = dot(perm, total.astype(BF16)).astype(BF16)
    ring = []
    for i, (a, b, t) in enumerate(around):
        at = pl.ds((0, 64, 128)[b], 64)
        ring.append(remote(zc.at[1, pl.ds(0, 64)], zc.at[1 - a, at], nsend.at[i], nrecv.at[i], t))
    for copy in ring:
        copy.start()
    sends += ring
    for copy in ring:
        copy.wait_recv()

    cell = lax.broadcasted_iota(jnp.int32, (PITCH, 256), 0)
    across = ((cell >= LEAD) | (r > 0)) & ((cell < LEAD + 128) | (r < NR - 1))

    def on_grid(values, y):
        here = 16 * g + y
        return jnp.where(across & (here >= 0) & (here < 16 * NG), values, 0.0)

    def first_hidden(y0, a0, count, band):
        size = count * PITCH
        u = p1[rows_at((y0 + 2) * PITCH, size), :] + dot(amat[rows_at(a0 * PITCH, size), :], zc[band])
        u = silu(u)
        for i in range(count):
            cells = on_grid(u[i * PITCH : (i + 1) * PITCH], y0 + i)
            xm[rows_at((y0 + 2 + i) * PITCH, PITCH), :] = spread3(cells)

    lax.fori_loop(0, 4, lambda i, _: (first_hidden(4 * i, 4 * i, 4, 1), 0)[1], 0)
    first_hidden(-2, 14, 2, 0)
    first_hidden(16, 0, 2, 2)

    def second_hidden(i, _):
        y0 = 3 * i
        parts = [xm[rows_at((y0 + a) * PITCH, 3 * PITCH), :] for a in range(3)]
        u = silu(dot_nt(jnp.concatenate(parts, axis=1), w2[...]))
        for j in range(3):
            cells = on_grid(u[j * PITCH : (j + 1) * PITCH], y0 + j - 1)
            x2[rows_at((y0 + j) * PITCH, PITCH), :] = cells.astype(BF16)
        return 0

    lax.fori_loop(0, 6, second_hidden, 0)

    def last_conv(i, _):
        y0 = 4 * i
        parts = [x2[rows_at((y0 + a) * PITCH, 4 * PITCH), :] for a in range(3)]
        terms = dot_nt(jnp.concatenate(parts, axis=1), w3[...])
        for j in range(4):
            t = terms[j * PITCH : (j + 1) * PITCH]
            total = pltpu.roll(t[:, 0:128], 1, 0) + t[:, 128:256] + pltpu.roll(t[:, 256:384], PITCH - 1, 0)
            at = pl.ds(y0 + j, 128, stride=16)
            ost[at, :] = st32[at, :] + total[LEAD : LEAD + 128].T
        return 0

    lax.fori_loop(0, 4, last_conv, 0)
    store_r = pltpu.make_async_copy(ost.at[pl.ds(0, 1584)], rnext_hbm, osem.at[1])
    store_r.start()
    for copy in sends + forwards:
        copy.wait_send()
    store_g.wait()
    store_r.wait()


def on_device(
    global_state, norm_gain, qkv_weight, out_weight, position_bias, regional_state,
    conv_state, cond_weight, conv_mid, conv_out, blocks, sources, block_ids, shift_offset,
):
    vm, anywhere = pl.BlockSpec(memory_space=pltpu.VMEM), pl.BlockSpec(memory_space=pl.ANY)
    dma = pltpu.SemaphoreType.DMA
    scratch = [
        ((16, 64, 512), BF16), ((99, 16, 128), BF16), ((512, 1536), BF16), ((512, 512), BF16),
        ((8, 128, 128), F32), ((9, 256, 99), BF16), ((256, 512), BF16), ((9, 256, 256), BF16),
        ((9, 99, 256), BF16), ((64, 2048), BF16),
        ((8, 64, 512), BF16), ((8, 64, 512), BF16), ((8, 64, 512), BF16),
        ((8, 128), jnp.int32), ((8, 2, 8, 128), jnp.int32),
        ((512, 512), BF16), ((512, 512), BF16), ((512, 1536), BF16), ((512, 512), BF16),
        ((24, 64, 512), BF16), ((16, 64, 512), BF16), ((1024, 256), BF16),
        ((2, 512, 1024), BF16), ((2, 512, 256), BF16), ((512, 256), BF16),
        ((7, 64, 256), BF16), ((3, 256, 256), BF16),
        ((2048, 128), F32), ((2, 128, 128), F32),
        ((128, 128), BF16), ((128, 128), BF16), ((128, 128), BF16), ((128, 128), BF16),
        ((16 * PITCH, 128), F32), ((22 * PITCH, 384), BF16),
        ((3 * PITCH, 128), BF16), ((3 * PITCH, 128), BF16), ((20 * PITCH, 256), F32),
        ((256, 1152), BF16), ((256, 2304), BF16), ((384, 768), BF16),
        ((16 * PITCH, 256), BF16), ((20 * PITCH, 768), BF16), ((18 * PITCH, 256), BF16),
        ((2048, 128), F32),
    ]
    counts = [10, 4, 4, 4, 4, 2, 2, 2, 2, 8, 8, 0, 0, 7, 7, 8, 8, 2]
    gnext, rnext = pl.pallas_call(
        body,
        out_shape=[
            jax.ShapeDtypeStruct((16, 64, 512), BF16),
            jax.ShapeDtypeStruct((1584, 128), F32),
        ],
        in_specs=[pl.BlockSpec(memory_space=pltpu.SMEM)] + [vm] * 3 + [anywhere] * 10,
        out_specs=[anywhere, anywhere],
        scratch_shapes=[pltpu.VMEM(*s) for s in scratch] + [dma((n,)) if n else dma for n in counts],
        compiler_params=pltpu.CompilerParams(
            collective_id=0, has_side_effects=True, vmem_limit_bytes=60 * 2**20
        ),
    )(
        shift_offset, sources.reshape(1, 64), block_ids.reshape(1, 64), norm_gain.reshape(1, 512),
        global_state, regional_state, qkv_weight, out_weight, position_bias,
        conv_state, cond_weight, conv_mid, conv_out, blocks,
    )
    return gnext, rnext.reshape(99, 16, 128)


def solution(mesh):
    return jax.shard_map(
        on_device,
        mesh=mesh,
        in_specs=(
            P("glob", "reg", None),
            P(), P(), P(), P(),
            P(None, "glob", "reg"),
            P(), P(), P(), P(), P(),
            P("glob", "reg", None),
            P("glob", "reg", None),
            P(),
        ),
        out_specs=(P("glob", "reg", None), P(None, "glob", "reg")),
        check_vma=False,
    )
```

profile of v0, /device:TPU:0, one launch (start us, length us, event | category | flops | bytes accessed | tf_op | source)
XLA Modules:
  0.0 69.2 jit_solution(2253465070246347191)
XLA Ops:
  1.3 2.1 %copy.16.cs_hbm = bf16[9,256,99]{2,1,0:T(8,128)(2,1)} copy(bf16[9,256,99]{1,2,0:T(8,128)(2,1)} %param.20) | data formatting | bytes 912384 | tf_op args[6]
  3.4 62.6 %shard_map.149 = (bf16[16,64,512]{2,1,0:T(8,128)(2,1)}, f32[1584,128]{1,0:T(8,128)}) custom-call(s32[1]{0:T(128)S(6)} %copy.19.shift_ref, s32[1,64]{1,0:T(1,128)} %bitcast.6, s32[1,64]{1,0:T(1,128)} %bitcast.7, f32[1,512]{1,0:T(1,128)} %bitcast.5, bf16[16,64,512]{2,1,0:T(8,128)(2,1)} %gs_hbm.1, bf16[99,16,128]{2,1,0:T(8,128)(2,1)} %rs_hbm.1, ...), custom_call_target="tpu_custom_call" | custom-call | tf_op jit(solution)/shard_map/pallas_call | solution.py:406
  66.0 0.0 copy-start
  66.0 2.4 %copy.20 = bf16[16,64,512]{2,1,0:T(8,128)(2,1)} copy(bf16[16,64,512]{2,1,0:T(8,128)(2,1)} %get-tuple-element.8) | data formatting | bytes 2097152
  68.4 0.0 copy-done
  68.4 0.9 %copy.21 = f32[99,16,128]{2,1,0:T(8,128)} copy(f32[99,16,128]{2,1,0:T(8,128)S(1)} %bitcast.4) | data formatting | bytes 1622016
Async XLA Ops:
  66.0 2.4 %copy-start = (f32[1584,128]{1,0:T(8,128)S(1)}, f32[1584,128]{1,0:T(8,128)}, u32[]{:S(2)}) copy-start(f32[1584,128]{1,0:T(8,128)} %get-tuple-element.5) | copy-start | bytes 2433028
where the time goes:
time: 69.5 us; the launch traced here: 69.2 us
  Pallas kernels  62.6 us (90%)
  local copies, waits for them, and re-layouts  5.36 us (8%)
  between operations  1.29 us (2%)
    pallas_call x1, Pallas kernels, on_device(): pl.pallas_call(body, out_shape=[jax.ShapeDtypeStruct((16, 64, 512), BF16)...  62.6 us
    unnamed x5, local copies, waits for them, and re-layouts  5.36 us

commit v1 on v0

v1 whole, which is shorter than its diff:
```python
import jax
import jax.numpy as jnp
from jax import lax
from jax.experimental import pallas as pl
from jax.experimental.pallas import tpu as pltpu
from jax.sharding import PartitionSpec as P

MESH = pl.DeviceIdType.MESH
F32 = jnp.float32
BF16 = jnp.bfloat16
NG, NR = 8, 16
PITCH, LEAD = 144, 8
NT = (((1,), (1,)), ((), ()))


def dot(a, b):
    return jnp.dot(a, b, preferred_element_type=F32)


def dot_nt(a, b):
    return lax.dot_general(a, b, NT, preferred_element_type=F32)


def silu(u):
    half = 0.5 * u
    return half + half * jnp.tanh(half)


def rows_at(index, count):
    return pl.ds(pl.multiple_of(index, 16), count)


def body(
    shift_ref, src_ref, bid_ref, gain_ref,
    gs_hbm, rs_hbm, qkvw_hbm, outw_hbm, bias_hbm, cs_hbm, cw_hbm, cm_hbm, co_hbm, blk_hbm,
    gnext_hbm, rnext_hbm,
    own, rsv, qkvw, outw, bias, csv, cw, cmv, cov, blk,
    sb, pb, fb, xb, hb, slab, sg, xn, qk, qkv, qp, kv, biasr, span, packed, onext, yv, sel, zpart, zs, zr, z2, zc, cout, cin,
    st32, edge, el, er, rl, rr, xf, x3, hu, hd, p1, w1, w2, w3, amat, xm, x2, pt, ost,
    lsem, psend, precv, fsend, frecv, esend, erecv, hsend, hrecv, gsend, grecv,
    asend, arecv, bsend, brecv, nsend, nrecv, osem,
):
    g = lax.axis_index("glob")
    r = lax.axis_index("reg")
    odd = lax.rem(g, 2)
    core = lax.rem(r, 2)
    chip = r // 2
    shift = shift_ref[0]
    partner = (g + 1 - 2 * odd, r)
    ahead = (lax.rem(g + 2 - 4 * odd + NG, NG), r)
    behind = (lax.rem(g - 2 + 4 * odd + NG, NG), r)
    other = (lax.rem(g - 1 + 2 * odd + NG, NG), r)
    mate = (g, r + 1 - 2 * core)
    far = (g, lax.rem(r - 1 + 2 * core + NR, NR))
    up, down = (lax.rem(g + NG - 1, NG), r), (lax.rem(g + 1, NG), r)
    left, right = (g, lax.rem(r + NR - 1, NR)), (g, lax.rem(r + 1, NR))
    chips = [(g, lax.rem(r + 2 * d, NR)) for d in range(1, 8)]
    around = [
        (a, b, (lax.rem(g + a + NG, NG), lax.rem(r + b + NR, NR)))
        for a in (-1, 0, 1) for b in (-1, 0, 1) if (a, b) != (0, 0)
    ]

    bar = pltpu.get_barrier_semaphore()
    greet = [partner, other, ahead, behind, mate, far] + chips + [t for a, b, t in around if a and b]
    for target in greet:
        pl.semaphore_signal(bar, inc=1, device_id=target, device_id_type=MESH)
    local = [
        (gs_hbm, own), (rs_hbm, rsv), (qkvw_hbm, qkvw), (bias_hbm, bias), (outw_hbm, outw),
        (blk_hbm, blk), (cs_hbm, csv), (cw_hbm, cw), (cm_hbm, cmv), (co_hbm, cov),
    ]
    loads = [pltpu.make_async_copy(a, b, lsem.at[i]) for i, (a, b) in enumerate(local)]
    for copy in loads:
        copy.start()

    def remote(src, dst, ssem, rsem, target):
        return pltpu.make_async_remote_copy(
            src_ref=src, dst_ref=dst, send_sem=ssem, recv_sem=rsem,
            device_id=target, device_id_type=MESH,
        )

    loads[0].wait()
    for i in range(4):
        sb[i] = own[i + jnp.where(i < 8 - shift, 0, 8)]
    slab[...] = jnp.zeros(slab.shape, jnp.int32)
    slab[0:1, 0:64] = src_ref[...]
    sg[chip, core] = slab[...]
    zc[1, 192:256, :] = jnp.zeros((64, 256), BF16)
    for band in (0, 2):
        zc[band, 64:256, :] = jnp.zeros((192, 256), BF16)
    pl.semaphore_wait(bar, len(greet))

    firsts, seconds, forwards, mergeds = [], [], [], []
    for c in range(2):
        at, late = pl.ds(2 * c, 2), pl.ds(4 + 2 * c, 2)
        firsts.append(remote(sb.at[at], pb.at[at], psend.at[c], precv.at[c], partner))
        seconds.append(remote(own.at[pl.ds(4 + 2 * c + 8 * odd, 2)], xb.at[at], psend.at[2 + c], precv.at[2 + c], behind))
        forwards.append(remote(pb.at[at], fb.at[at], fsend.at[c], frecv.at[c], ahead))
        mergeds.append(remote(sb.at[late], hb.at[late], fsend.at[2 + c], frecv.at[2 + c], partner))
    for c in range(2):
        firsts[c].start()
        seconds[c].start()
    mate_slab = remote(slab, sg.at[chip, core], gsend.at[0], grecv.at[0], mate)
    mate_slab.start()
    sends = firsts + seconds + forwards + mergeds + [mate_slab]

    def pass_on(c):
        firsts[c].wait_recv()
        forwards[c].start()
        seconds[c].wait_recv()
        for i in range(4 + 2 * c, 6 + 2 * c):
            for_partner = own[i + 8 * (1 - odd)]
            from_behind = xb[i - 4]
            up_row = i < 8 - shift
            sb[i] = jnp.where(jnp.where(odd == 1, jnp.logical_not(up_row), up_row), from_behind, for_partner)
        mergeds[c].start()

    loads[1].wait()
    st32[0:1584, :] = rsv[...].reshape(1584, 128).astype(F32)
    st32[1584:2048, :] = jnp.zeros((464, 128), F32)

    def turn(y, _):
        cells = st32[pl.ds(y, 128, stride=16), :].T
        xf[pl.ds(pl.multiple_of(y * PITCH + LEAD, 8), 128), :] = cells
        at = pl.ds(pl.multiple_of(y * 8, 8), 8)
        edge[0, at, :] = cells[0:8]
        edge[1, at, :] = cells[120:128]
        return 0

    lax.fori_loop(0, 16, turn, 0, unroll=True)
    el[...] = edge[0].astype(BF16)
    er[...] = edge[1].astype(BF16)
    edges = [
        remote(el, rr, esend.at[0], erecv.at[0], left),
        remote(er, rl, esend.at[1], erecv.at[1], right),
    ]
    for copy in edges:
        copy.start()
    sends += edges

    mate_slab.wait_recv()
    slabs = [
        remote(sg.at[chip], sg.at[chip], gsend.at[1 + i], grecv.at[1 + i], t) for i, t in enumerate(chips)
    ]
    for copy in slabs:
        copy.start()
    sends += slabs

    low = lax.broadcasted_iota(jnp.int32, (128, 128), 1) < 64
    upward = [i < 8 - shift for i in range(8)]
    packed_row = [i + jnp.where(upward[i], 0, 8) for i in range(8)]

    def project(tokens, at, first):
        count = tokens.shape[0] * 64
        for w in range(0, count, 128):
            values = tokens[w // 64 : w // 64 + 2].reshape(128, 512).astype(F32)
            center = values - jnp.mean(values, axis=-1, keepdims=True)
            spread = jnp.mean(center * center, axis=-1, keepdims=True)
            xn[w : w + 128, :] = (center * lax.rsqrt(spread + 1e-05) * gain_ref[...]).astype(BF16)
        for n in range(first, 3):
            part = dot(xn[0:count, :], qkvw[:, n * 512 : n * 512 + 512]).astype(BF16)
            if n == 0:
                part = (part * 0.125).astype(BF16)
            qk[at : at + count // 64, :, n * 512 : n * 512 + 512] = part.reshape(count // 64, 64, 512)

    places = [(w, hp) for w in range(4) for hp in range(4)]

    def two_heads(q):
        zero = jnp.zeros_like(q)
        return jnp.concatenate([jnp.where(low, q, zero), jnp.where(low, zero, q)], axis=0)

    def keep(w, hp, mixed):
        for j in range(8):
            span[j, w * 16 : w * 16 + 16, hp * 128 : hp * 128 + 128] = mixed[j * 16 : j * 16 + 16]

    def attend_inner():
        for j in range(8):
            row = qk[8 - shift + j]
            for w in range(4):
                qkv[w * 128 + j * 16 : w * 128 + j * 16 + 16, :] = row[w * 16 : w * 16 + 16, :]
        ones = jnp.ones((128, 128), BF16)
        scores = []
        for w, hp in places:
            q = qkv[w * 128 : w * 128 + 128, hp * 128 : hp * 128 + 128]
            key = qkv[w * 128 : w * 128 + 128, 512 + hp * 128 : 512 + hp * 128 + 128]
            scores.append(dot_nt(two_heads(q), key))
        weights = []
        for (w, hp), score in zip(places, scores):
            score = score + bias[2 * hp : 2 * hp + 2].reshape(256, 128)
            weights.append(jnp.exp(score - jnp.max(score, axis=-1, keepdims=True)).astype(BF16))
        sums = []
        for (w, hp), weight in zip(places, weights):
            val = qkv[w * 128 : w * 128 + 128, 1024 + hp * 128 : 1024 + hp * 128 + 128]
            sums.append(dot(weight, jnp.concatenate([val, ones], axis=1)))
        for (w, hp), both in zip(places, sums):
            top = jnp.where(low, both[0:128, 0:128], both[128:256, 0:128])
            under = jnp.where(low, both[0:128, 128:256], both[128:256, 128:256])
            keep(w, hp, (top / under).astype(BF16))

    def cross_setup():
        for i in range(8):
            row = qk[packed_row[i], :, 0:512]
            for w in range(4):
                qp[w * 128 + i * 16 : w * 128 + i * 16 + 16, :] = row[w * 16 : w * 16 + 16, :]
        first = lax.broadcasted_iota(jnp.int32, (16, 128), 1) // 16 < shift
        for i in range(8):
            above = jnp.where((g == 0) & first, -jnp.inf, 0.0)
            below = jnp.where((g < NG - 1) | first, 0.0, -jnp.inf)
            absent = jnp.where(upward[i], above, below).astype(F32)
            at = i + shift - jnp.where(i + shift >= 8, 8, 0)
            for h in range(8):
                biasr[h, i * 16 : i * 16 + 16, :] = bias[h, at] + absent

    def attend_cross():
        for j in range(8):
            rows = (
                qk[jnp.where(j < shift, 24 - shift + j, j - shift), :, 512:1536],
                qk[jnp.where(j < shift, 16 - shift + j, 16 + j - shift), :, 512:1536],
            )
            for k in range(2):
                for w in range(4):
                    at = w * 256 + k * 128 + j * 16
                    kv[at : at + 16, :] = rows[k][w * 16 : w * 16 + 16, :]
        upper = (lax.broadcasted_iota(jnp.int32, (256, 128), 0) // 16) % 8 < 8 - shift
        scores = []
        for w, hp in places:
            q = qp[w * 128 : w * 128 + 128, hp * 128 : hp * 128 + 128]
            scores.append(dot_nt(two_heads(q), kv[w * 256 : w * 256 + 256, hp * 128 : hp * 128 + 128]))
        weights, sums = [], []
        for (w, hp), score in zip(places, scores):
            score = jnp.where(upper, score[:, 0:128], score[:, 128:256])
            score = score + biasr[2 * hp : 2 * hp + 2].reshape(256, 128)
            weight = jnp.exp(score - jnp.max(score, axis=-1, keepdims=True))
            sums.append(jnp.sum(weight, axis=-1, keepdims=True))
            weights.append(weight.astype(BF16))
        mixes = []
        for (w, hp), weight in zip(places, weights):
            cols = slice(512 + hp * 128, 512 + hp * 128 + 128)
            vals = [kv[w * 256 + k * 128 : w * 256 + k * 128 + 128, cols] for k in range(2)]
            mixes.append(dot(weight, jnp.concatenate(vals, axis=1)))
        for (w, hp), mix, total in zip(places, mixes, sums):
            mix = jnp.where(upper, mix[:, 0:128], mix[:, 128:256]) / total
            keep(w, hp, jnp.where(low, mix[0:128], mix[128:256]).astype(BF16))

    def update(at, index):
        change = dot(span[...].reshape(512, 512), outw[...])
        for i in range(8):
            mine = own[index(i)].astype(F32) + change[i * 64 : i * 64 + 64]
            packed[at + i] = mine.astype(BF16)
        tokens = packed[at : at + 8].reshape(512, 512)
        yv[at * 64 : at * 64 + 512, :] = dot_nt(tokens, cw[...]).astype(BF16)

    loads[2].wait()
    project(own[...], 0, 0)
    pass_on(0)
    for i in range(3, 10):
        loads[i].wait()
    attend_inner()
    update(8, lambda j: 8 - shift + j)
    cross_setup()

    for o in range(9):
        w1[o * 128 : o * 128 + 128, :] = jnp.concatenate(
            [csv[o].astype(F32), jnp.zeros((29, 256), F32)], axis=0
        ).astype(BF16)
        w2[:, o * 256 : o * 256 + 256] = cmv[o]
        a, b = o // 3, o % 3
        w3[b * 128 : b * 128 + 128, a * 256 : a * 256 + 256] = jnp.concatenate(
            [cov[o].astype(F32), jnp.zeros((29, 256), F32)], axis=0
        ).astype(BF16)

    def interpolation(y, _):
        part = blk[:, pl.ds(pl.multiple_of(y * 128, 128), 128)].astype(F32)
        cells = jnp.concatenate([part, jnp.zeros((64, 128), F32)], axis=0).T
        main = jnp.concatenate(
            [pltpu.roll(cells[120:128], 64, 1), cells, jnp.zeros((8, 128), F32)], axis=0
        )
        side = jnp.concatenate([jnp.zeros((136, 128), F32), cells[0:8]], axis=0)
        amat[rows_at(y * PITCH, PITCH), :] = jnp.concatenate([main, side], axis=1).astype(BF16)
        return 0

    lax.fori_loop(0, 16, interpolation, 0, unroll=True)
    pass_on(1)

    for copy in edges:
        copy.wait_recv()
    edge[0] = jnp.where(r > 0, rl[...].astype(F32), 0.0)
    edge[1] = jnp.where(r < NR - 1, rr[...].astype(F32), 0.0)

    def spread3(cells):
        width = cells.shape[0]
        return jnp.concatenate([pltpu.roll(cells, 1, 0), cells, pltpu.roll(cells, width - 1, 0)], axis=1).astype(BF16)

    def frame(y, _):
        at = pl.ds(pl.multiple_of(y * 8, 8), 8)
        main = xf[pl.ds(pl.multiple_of(y * PITCH + LEAD, 8), 128), :]
        cells = jnp.concatenate([edge[0, at, :], main, edge[1, at, :]], axis=0)
        x3[rows_at((y + 3) * PITCH, PITCH), :] = spread3(cells)
        return 0

    lax.fori_loop(0, 16, frame, 0, unroll=True)
    borders = [
        remote(x3.at[pl.ds(3 * PITCH, 3 * PITCH), pl.ds(128, 128)], hd, hsend.at[0], hrecv.at[0], up),
        remote(x3.at[pl.ds(16 * PITCH, 3 * PITCH), pl.ds(128, 128)], hu, hsend.at[1], hrecv.at[1], down),
    ]

    def first_conv(y0, count):
        parts = [x3[rows_at((y0 + a) * PITCH, count * PITCH), :] for a in range(3)]
        p1[rows_at(y0 * PITCH, count * PITCH), :] = dot(jnp.concatenate(parts, axis=1), w1[...])

    lax.fori_loop(0, 2, lambda i, _: (first_conv(3 + 7 * i, 7), 0)[1], 0, unroll=True)

    for copy in slabs:
        copy.wait_recv()
    ids = sg[...].reshape(128, 128)[0:128]
    ids = jnp.concatenate([ids[8 * j : 8 * j + 1] for j in range(16)], axis=0)
    row = lax.shift_right_logical(ids, 10) - 16 * g
    col = jnp.bitwise_and(ids, 1023) - 64 * r
    row = jnp.where(row < 8 - shift, row, jnp.where(row >= 16 - shift, row - 8, row + shift))
    token = jnp.where((col >= 0) & (col < 64), row * 64 + col, -1).astype(F32)
    token = jnp.concatenate([token, jnp.zeros((112, 128), F32)], axis=0).T
    position = lax.broadcasted_iota(jnp.int32, (64, 1024), 1).astype(F32)
    for j in range(16):
        hit = token[0:64, j : j + 1] == position
        sel[j % 2, (j // 2) * 64 : (j // 2) * 64 + 64, :] = jnp.where(hit, 1.0, 0.0).astype(BF16)
    for half in range(2):
        zpart[half] = dot(sel[half, :, 512:1024], yv[512:1024, :])
    slots = lax.broadcasted_iota(jnp.int32, (64, 64), 0)
    perm = jnp.where(slots == bid_ref[...], 1.0, 0.0).astype(BF16)

    for copy in forwards + mergeds:
        copy.wait_recv()
    for copy in borders:
        copy.start()
    sends += borders
    for i in range(4):
        hb[i] = jnp.where(jnp.where(odd == 1, upward[i], jnp.logical_not(upward[i])), fb[i], pb[i])
    project(hb[...], 16, 1)
    attend_cross()

    update(0, lambda i: packed_row[i])

    def contribution(half):
        zs[half] = (zpart[half] + dot(sel[half, :, 0:512], yv[0:512, :])).astype(BF16)

    contribution(1 - core)
    to_mate = remote(zs.at[1 - core], zr, asend, arecv, mate)
    to_mate.start()
    contribution(core)
    for i in range(16):
        onext[i] = packed[jnp.where(i < 8 - shift, i, jnp.where(i >= 16 - shift, i - 8, i + shift))]
    store_g = pltpu.make_async_copy(onext, gnext_hbm, osem.at[0])
    store_g.start()
    to_mate.wait()
    zs[core] = zs[core] + zr[...]
    tiles = []
    for i, t in enumerate(chips):
        q = lax.rem(chip + i + 1, 8)
        tiles.append(remote(zs.at[core, rows_at(q * 64, 64)], z2.at[i], bsend.at[i], brecv.at[i], t))
    for copy in tiles:
        copy.start()
    for copy in borders:
        copy.wait_recv()
    for a in range(3):
        at = pl.ds(a * PITCH, PITCH)
        x3[a * PITCH : (a + 1) * PITCH, :] = spread3(jnp.where(g > 0, hu[at, :].astype(F32), 0.0))
        x3[(19 + a) * PITCH : (20 + a) * PITCH, :] = spread3(jnp.where(g < NG - 1, hd[at, :].astype(F32), 0.0))
    lax.fori_loop(0, 2, lambda i, _: (first_conv(17 * i, 3), 0)[1], 0, unroll=True)
    total = zs[core, rows_at(chip * 64, 64), :].astype(F32)
    for copy in tiles:
        copy.wait()
    for i in range(7):
        total = total + z2[i].astype(F32)
    zc[1, 0:64, :] = dot(perm, total.astype(BF16)).astype(BF16)
    corner_rows = [amat[y * PITCH + at : y * PITCH + at + 16, 0:64] for y in (0, 1, 14, 15) for at in (0, PITCH - 16)]
    corners = dot(jnp.concatenate(corner_rows, axis=0), zc[1, 0:64])
    for i in range(4):
        at = [(4 * (i // 2) + 2 * n + i % 2) * 16 + 8 * (1 - i % 2) for n in range(2)]
        cout[i] = jnp.concatenate([corners[at[0] : at[0] + 8], corners[at[1] : at[1] + 8]], axis=0).astype(BF16)
    ring = []
    for i, (a, b, t) in enumerate(around):
        if a and b:
            here, there = (1 + a) + (1 + b) // 2, (1 - a) + (1 - b) // 2
            ring.append(remote(cout.at[here], cin.at[there], nsend.at[i], nrecv.at[i], t))
        else:
            at = pl.ds((0, 64, 128)[b], 64)
            ring.append(remote(zc.at[1, pl.ds(0, 64)], zc.at[1 - a, at], nsend.at[i], nrecv.at[i], t))
    for copy in ring:
        copy.start()
    sends += ring

    cell = lax.broadcasted_iota(jnp.int32, (PITCH, 256), 0)
    across = ((cell >= LEAD) | (r > 0)) & ((cell < LEAD + 128) | (r < NR - 1))

    def on_grid(values, y):
        here = 16 * g + y
        return jnp.where(across & (here >= 0) & (here < 16 * NG), values, 0.0)

    for y0 in range(0, 16, 4):
        size = 4 * PITCH
        at = pl.ds(y0 * PITCH, size)
        u = p1[(y0 + 2) * PITCH : (y0 + 2) * PITCH + size, :] + dot(amat[at, 0:64], zc[1, 0:64])
        u = silu(u)
        for i in range(4):
            xm[(y0 + 2 + i) * PITCH : (y0 + 3 + i) * PITCH, :] = spread3(u[i * PITCH : (i + 1) * PITCH])

    def second_inner(y0, count):
        parts = [
            jnp.concatenate([xm[(y0 + i + a) * PITCH + 16 : (y0 + i + a) * PITCH + 128, :] for i in range(count)], axis=0)
            for a in range(3)
        ]
        u = silu(dot_nt(jnp.concatenate(parts, axis=1), w2[...])).astype(BF16)
        for i in range(count):
            x2[(y0 + i) * PITCH + 16 : (y0 + i) * PITCH + 128, :] = u[i * 112 : i * 112 + 112]

    second_inner(2, 7)
    second_inner(9, 7)

    def last_terms(cells):
        parts = [jnp.concatenate([x2[(y + a) * PITCH + p : (y + a) * PITCH + p + n, :] for y, p, n in cells], axis=0) for a in range(3)]
        terms = dot_nt(jnp.concatenate(parts, axis=1), w3[...])
        start = 0
        for y, p, n in cells:
            pt[y * PITCH + p : y * PITCH + p + n, :] = terms[start : start + n]
            start += n

    last_terms([(y, 16, 112) for y in range(2, 8)])
    last_terms([(y, 16, 112) for y in range(8, 14)])

    for copy in ring:
        copy.wait_recv()

    def first_rows(y0, a0, band):
        size = 2 * PITCH
        u = p1[(y0 + 2) * PITCH : (y0 + 2) * PITCH + size, :] + dot(amat[a0 * PITCH : a0 * PITCH + size, :], zc[band])
        ends = [cin[band + side].astype(F32) for side in range(2)]
        for i in range(2):
            cond = jnp.concatenate(
                [ends[0][8 * i : 8 * i + 8], jnp.zeros((128, 256), F32), ends[1][8 * i : 8 * i + 8]], axis=0
            )
            cells = on_grid(silu(u[i * PITCH : (i + 1) * PITCH] + cond), y0 + i)
            xm[(y0 + 2 + i) * PITCH : (y0 + 3 + i) * PITCH, :] = spread3(cells)

    first_rows(-2, 14, 0)
    first_rows(16, 0, 2)

    def edge_cells(ref, y, width):
        return [ref[y * PITCH : y * PITCH + width, :], ref[(y + 1) * PITCH - width : (y + 1) * PITCH, :]]

    own_part = jnp.concatenate([c for y in range(2, 18) for c in edge_cells(p1, y, 32)], axis=0)
    tile_part = jnp.concatenate([c for y in range(16) for c in edge_cells(amat, y, 32)], axis=0)
    u = silu(own_part + dot(tile_part, zc[1]))
    for y in range(16):
        for side in range(2):
            cells = u[(2 * y + side) * 32 : (2 * y + side) * 32 + 32]
            inside = across[0:32] if side == 0 else across[PITCH - 32 : PITCH]
            cells = spread3(jnp.where(inside, cells, 0.0))
            at = (y + 2) * PITCH + (0 if side == 0 else PITCH - 16)
            xm[at : at + 16, :] = cells[0:16] if side == 0 else cells[16:32]

    def second_rows(y0):
        parts = [xm[(y0 + a) * PITCH : (y0 + a + 2) * PITCH, :] for a in range(3)]
        u = silu(dot_nt(jnp.concatenate(parts, axis=1), w2[...]))
        for i in range(2):
            cells = on_grid(u[i * PITCH : (i + 1) * PITCH], y0 + i - 1)
            x2[(y0 + i) * PITCH : (y0 + i + 1) * PITCH, :] = cells.astype(BF16)

    second_rows(0)
    second_rows(16)
    parts = [jnp.concatenate([c for y in range(2, 16) for c in edge_cells(xm, y + a, 16)], axis=0) for a in range(3)]
    u = silu(dot_nt(jnp.concatenate(parts, axis=1), w2[...]))
    for y in range(2, 16):
        for side in range(2):
            cells = u[(y - 2) * 32 + side * 16 : (y - 2) * 32 + side * 16 + 16]
            inside = across[0:16] if side == 0 else across[PITCH - 16 : PITCH]
            at = y * PITCH + (0 if side == 0 else PITCH - 16)
            x2[at : at + 16, :] = jnp.where(inside, cells, 0.0).astype(BF16)

    last_terms([(y, 0, PITCH) for y in (0, 1, 14, 15)] + [(y, p, 16) for y in range(2, 14) for p in (0, PITCH - 16)])
    for y in range(16):
        t = pt[y * PITCH : (y + 1) * PITCH, :]
        total = pltpu.roll(t[:, 0:128], 1, 0) + t[:, 128:256] + pltpu.roll(t[:, 256:384], PITCH - 1, 0)
        at = pl.ds(y, 128, stride=16)
        ost[at, :] = st32[at, :] + total[LEAD : LEAD + 128].T
    store_r = pltpu.make_async_copy(ost.at[pl.ds(0, 1584)], rnext_hbm, osem.at[1])
    store_r.start()
    for copy in sends:
        copy.wait_send()
    store_g.wait()
    store_r.wait()


def hand_over(gnext_in, rnext_in, gnext_out, rnext_out, gbuf, rbuf, isem, osem):
    pairs = []
    for i in range(4):
        at, rows = pl.ds(4 * i, 4), pl.ds(400 * i, 400 if i < 3 else 384)
        for n, (a, b, c, part) in enumerate(((gnext_in, gbuf, gnext_out, at), (rnext_in, rbuf, rnext_out, rows))):
            first = pltpu.make_async_copy(a.at[part], b.at[part], isem.at[2 * i + n])
            pairs.append((first, pltpu.make_async_copy(b.at[part], c.at[part], osem.at[2 * i + n])))
    for first, _ in pairs:
        first.start()
    for first, second in pairs:
        first.wait()
        second.start()
    for _, second in pairs:
        second.wait()


def on_device(
    global_state, norm_gain, qkv_weight, out_weight, position_bias, regional_state,
    conv_state, cond_weight, conv_mid, conv_out, blocks, sources, block_ids, shift_offset,
):
    vm, anywhere = pl.BlockSpec(memory_space=pltpu.VMEM), pl.BlockSpec(memory_space=pl.ANY)
    dma = pltpu.SemaphoreType.DMA
    scratch = [
        ((16, 64, 512), BF16), ((99, 16, 128), BF16), ((512, 1536), BF16), ((512, 512), BF16),
        ((8, 8, 16, 128), F32), ((9, 99, 256), BF16), ((256, 512), BF16), ((9, 256, 256), BF16),
        ((9, 99, 256), BF16), ((64, 2048), BF16),
        ((8, 64, 512), BF16), ((4, 64, 512), BF16), ((4, 64, 512), BF16),
        ((4, 64, 512), BF16), ((8, 64, 512), BF16),
        ((8, 128), jnp.int32), ((8, 2, 8, 128), jnp.int32),
        ((1024, 512), BF16), ((24, 64, 1536), BF16), ((512, 1536), BF16),
        ((512, 512), BF16), ((1024, 1024), BF16), ((8, 128, 128), F32),
        ((8, 64, 512), BF16), ((16, 64, 512), BF16), ((16, 64, 512), BF16), ((1024, 256), BF16),
        ((2, 512, 1024), BF16), ((2, 512, 256), F32), ((2, 512, 256), BF16), ((512, 256), BF16),
        ((7, 64, 256), BF16), ((3, 256, 256), BF16), ((4, 16, 256), BF16), ((4, 16, 256), BF16),
        ((2048, 128), F32), ((2, 128, 128), F32),
        ((128, 128), BF16), ((128, 128), BF16), ((128, 128), BF16), ((128, 128), BF16),
        ((16 * PITCH, 128), F32), ((22 * PITCH, 384), BF16),
        ((3 * PITCH, 128), BF16), ((3 * PITCH, 128), BF16), ((20 * PITCH, 256), F32),
        ((1152, 256), BF16), ((256, 2304), BF16), ((384, 768), BF16),
        ((16 * PITCH, 256), BF16), ((20 * PITCH, 768), BF16), ((18 * PITCH, 256), BF16),
        ((16 * PITCH, 384), F32), ((2048, 128), F32),
    ]
    counts = [10, 4, 4, 4, 4, 2, 2, 2, 2, 8, 8, 0, 0, 7, 7, 8, 8, 2]
    gnext, rnext = pl.pallas_call(
        body,
        out_shape=[
            jax.ShapeDtypeStruct((16, 64, 512), BF16),
            jax.ShapeDtypeStruct((1584, 128), F32),
        ],
        in_specs=[pl.BlockSpec(memory_space=pltpu.SMEM)] + [vm] * 3 + [anywhere] * 10,
        out_specs=[anywhere, anywhere],
        scratch_shapes=[pltpu.VMEM(*s) for s in scratch] + [dma((n,)) if n else dma for n in counts],
        compiler_params=pltpu.CompilerParams(
            collective_id=0, has_side_effects=True, vmem_limit_bytes=60 * 2**20
        ),
    )(
        shift_offset, sources.reshape(1, 64), block_ids.reshape(1, 64), norm_gain.reshape(1, 512),
        global_state, regional_state, qkv_weight, out_weight, position_bias.reshape(8, 8, 16, 128),
        jnp.swapaxes(conv_state, 1, 2), cond_weight, conv_mid, conv_out, blocks,
    )
    gnext, rnext = pl.pallas_call(
        hand_over,
        out_shape=[
            jax.ShapeDtypeStruct((16, 64, 512), BF16),
            jax.ShapeDtypeStruct((1584, 128), F32),
        ],
        in_specs=[anywhere, anywhere],
        out_specs=[anywhere, anywhere],
        scratch_shapes=[pltpu.VMEM((16, 64, 512), BF16), pltpu.VMEM((1584, 128), F32), dma((8,)), dma((8,))],
    )(gnext, rnext)
    return gnext, rnext.reshape(99, 16, 128)


def solution(mesh):
    return jax.shard_map(
        on_device,
        mesh=mesh,
        in_specs=(
            P("glob", "reg", None),
            P(), P(), P(), P(),
            P(None, "glob", "reg"),
            P(), P(), P(), P(), P(),
            P("glob", "reg", None),
            P("glob", "reg", None),
            P(),
        ),
        out_specs=(P("glob", "reg", None), P(None, "glob", "reg")),
        check_vma=False,
    )
```

time: 69.5 us -> 49.7 us (0.72)
  Pallas kernels: 62.6 us -> 48.1 us
  local copies, waits for them, and re-layouts: 5.36 us -> 0 us
    pallas_call x1, Pallas kernels: 62.6 us -> 45.8 us  [on_device(): pl.pallas_call(body, out_shape=[jax.ShapeDtypeStruct((16, 64, 512), BF16)...]
    unnamed x5 -> x0, local copies, waits for them, and re-layouts: 5.36 us -> none
    pallas_call x0 -> x1, Pallas kernels: none -> 2.34 us  [on_device(): pl.pallas_call(hand_over, out_shape=[jax.ShapeDtypeStruct((16, 64, 512),...]
where the time goes in v1:
time: 49.7 us; the launch traced here: 49.6 us
  Pallas kernels  48.1 us (97%)
  between operations  1.45 us (3%)
    pallas_call x1, Pallas kernels, on_device(): pl.pallas_call(body, out_shape=[jax.ShapeDtypeStruct((16, 64, 512), BF16)...  45.8 us
    pallas_call x1, Pallas kernels, on_device(): pl.pallas_call(hand_over, out_shape=[jax.ShapeDtypeStruct((16, 64, 512),...  2.34 us

profile of v1, /device:TPU:0, one launch (start us, length us, event | category | flops | bytes accessed | tf_op | source)
XLA Modules:
  0.0 49.6 jit_solution(17274213654224134644)
XLA Ops:
  1.3 45.8 %shard_map.149 = (bf16[16,64,512]{2,1,0:T(8,128)(2,1)}, f32[1584,128]{1,0:T(8,128)}) custom-call(s32[1]{0:T(128)S(6)} %copy.16.shift_ref, s32[1,64]{1,0:T(1,128)} %bitcast.9, s32[1,64]{1,0:T(1,128)} %bitcast.10, f32[1,512]{1,0:T(1,128)} %bitcast.8, bf16[16,64,512]{2,1,0:T(8,128)(2,1)} %gs_hbm.1, bf16[99,16,128]{2,1,0:T(8,128)(2,1)} %rs_hbm.1, ...), custom_call_target="tpu_custom_call" | custom-call | tf_op jit(solution)/shard_map/pallas_call | solution.py:535
  47.1 2.3 %shard_map.150 = (bf16[16,64,512]{2,1,0:T(8,128)(2,1)}, f32[1584,128]{1,0:T(8,128)}) custom-call(bf16[16,64,512]{2,1,0:T(8,128)(2,1)} %get-tuple-element.6.gnext_in, f32[1584,128]{1,0:T(8,128)} %get-tuple-element.7.rnext_in), custom_call_target="tpu_custom_call" | custom-call | tf_op jit(solution)/shard_map/pallas_call | solution.py:552

commit v2 on v1

--- a/solution.py
+++ b/solution.py
@@ -38,7 +38,7 @@
     sb, pb, fb, xb, hb, slab, sg, xn, qk, qkv, qp, kv, biasr, span, packed, onext, yv, sel, zpart, zs, zr, z2, zc, cout, cin,
     st32, edge, el, er, rl, rr, xf, x3, hu, hd, p1, w1, w2, w3, amat, xm, x2, pt, ost,
     lsem, psend, precv, fsend, frecv, esend, erecv, hsend, hrecv, gsend, grecv,
-    asend, arecv, bsend, brecv, nsend, nrecv, osem,
+    asend, arecv, bsend, brecv, nsend, nrecv, osem, rounds,
 ):
     g = lax.axis_index("glob")
     r = lax.axis_index("reg")
@@ -49,9 +49,7 @@
     partner = (g + 1 - 2 * odd, r)
     ahead = (lax.rem(g + 2 - 4 * odd + NG, NG), r)
     behind = (lax.rem(g - 2 + 4 * odd + NG, NG), r)
-    other = (lax.rem(g - 1 + 2 * odd + NG, NG), r)
     mate = (g, r + 1 - 2 * core)
-    far = (g, lax.rem(r - 1 + 2 * core + NR, NR))
     up, down = (lax.rem(g + NG - 1, NG), r), (lax.rem(g + 1, NG), r)
     left, right = (g, lax.rem(r + NR - 1, NR)), (g, lax.rem(r + 1, NR))
     chips = [(g, lax.rem(r + 2 * d, NR)) for d in range(1, 8)]
@@ -61,9 +59,13 @@
     ]
 
     bar = pltpu.get_barrier_semaphore()
-    greet = [partner, other, ahead, behind, mate, far] + chips + [t for a, b, t in around if a and b]
+    greet = [partner, ahead, behind, mate, (g, lax.rem(r + 4, NR)), (g, lax.rem(r + 12, NR)), (g, r + 2 - 4 * lax.rem(chip, 2))]
     for target in greet:
         pl.semaphore_signal(bar, inc=1, device_id=target, device_id_type=MESH)
+    def tell(i):
+        for target in greet:
+            pl.semaphore_signal(rounds.at[i], inc=1, device_id=target, device_id_type=MESH)
+
     local = [
         (gs_hbm, own), (rs_hbm, rsv), (qkvw_hbm, qkvw), (bias_hbm, bias), (outw_hbm, outw),
         (blk_hbm, blk), (cs_hbm, csv), (cw_hbm, cw), (cm_hbm, cmv), (co_hbm, cov),
@@ -102,6 +104,7 @@
     mate_slab = remote(slab, sg.at[chip, core], gsend.at[0], grecv.at[0], mate)
     mate_slab.start()
     sends = firsts + seconds + forwards + mergeds + [mate_slab]
+    tell(0)
 
     def pass_on(c):
         firsts[c].wait_recv()
@@ -133,17 +136,8 @@
         remote(el, rr, esend.at[0], erecv.at[0], left),
         remote(er, rl, esend.at[1], erecv.at[1], right),
     ]
-    for copy in edges:
-        copy.start()
-    sends += edges
-
-    mate_slab.wait_recv()
-    slabs = [
-        remote(sg.at[chip], sg.at[chip], gsend.at[1 + i], grecv.at[1 + i], t) for i, t in enumerate(chips)
-    ]
-    for copy in slabs:
-        copy.start()
-    sends += slabs
+    pl.semaphore_wait(rounds.at[0], len(greet))
+    tell(1)
 
     low = lax.broadcasted_iota(jnp.int32, (128, 128), 1) < 64
     upward = [i < 8 - shift for i in range(8)]
@@ -252,11 +246,24 @@
     loads[2].wait()
     project(own[...], 0, 0)
     pass_on(0)
+    pl.semaphore_wait(rounds.at[1], len(greet))
+    tell(2)
+    for copy in edges:
+        copy.start()
+    mate_slab.wait_recv()
+    slabs = [
+        remote(sg.at[chip], sg.at[chip], gsend.at[1 + i], grecv.at[1 + i], t) for i, t in enumerate(chips)
+    ]
+    for copy in slabs:
+        copy.start()
+    sends += edges + slabs
     for i in range(3, 10):
         loads[i].wait()
     attend_inner()
     update(8, lambda j: 8 - shift + j)
     cross_setup()
+    pl.semaphore_wait(rounds.at[2], len(greet))
+    tell(3)
 
     for o in range(9):
         w1[o * 128 : o * 128 + 128, :] = jnp.concatenate(
@@ -326,6 +333,8 @@
         zpart[half] = dot(sel[half, :, 512:1024], yv[512:1024, :])
     slots = lax.broadcasted_iota(jnp.int32, (64, 64), 0)
     perm = jnp.where(slots == bid_ref[...], 1.0, 0.0).astype(BF16)
+
+    pl.semaphore_wait(rounds.at[3], len(greet))
 
     for copy in forwards + mergeds:
         copy.wait_recv()
@@ -540,7 +549,7 @@
         ],
         in_specs=[pl.BlockSpec(memory_space=pltpu.SMEM)] + [vm] * 3 + [anywhere] * 10,
         out_specs=[anywhere, anywhere],
-        scratch_shapes=[pltpu.VMEM(*s) for s in scratch] + [dma((n,)) if n else dma for n in counts],
+        scratch_shapes=[pltpu.VMEM(*s) for s in scratch] + [dma((n,)) if n else dma for n in counts] + [pltpu.SemaphoreType.REGULAR((4,))],
         compiler_params=pltpu.CompilerParams(
             collective_id=0, has_side_effects=True, vmem_limit_bytes=60 * 2**20
         ),

time: 49.7 us -> 49.1 us (0.988); the launches traced: 49.6 us -> 48.3 us
  Pallas kernels: 48.1 us -> 46.9 us
    pallas_call x1, Pallas kernels: 45.8 us -> 44.5 us  [on_device(): pl.pallas_call(body, out_shape=[jax.ShapeDtypeStruct((16, 64, 512), BF16)...]
where the time goes in v2:
time: 49.1 us; the launch traced here: 48.3 us
  Pallas kernels  46.9 us (96%)
  between operations  1.45 us (3%)
    pallas_call x1, Pallas kernels, on_device(): pl.pallas_call(body, out_shape=[jax.ShapeDtypeStruct((16, 64, 512), BF16)...  44.5 us
    pallas_call x1, Pallas kernels, on_device(): pl.pallas_call(hand_over, out_shape=[jax.ShapeDtypeStruct((16, 64, 512),...  2.34 us

profile of v2, /device:TPU:0, one launch (start us, length us, event | category | flops | bytes accessed | tf_op | source)
XLA Modules:
  0.0 48.3 jit_solution(16275771606203298662)
XLA Ops:
  1.3 44.5 %shard_map.149 = (bf16[16,64,512]{2,1,0:T(8,128)(2,1)}, f32[1584,128]{1,0:T(8,128)}) custom-call(s32[1]{0:T(128)S(6)} %copy.16.shift_ref, s32[1,64]{1,0:T(1,128)} %bitcast.9, s32[1,64]{1,0:T(1,128)} %bitcast.10, f32[1,512]{1,0:T(1,128)} %bitcast.8, bf16[16,64,512]{2,1,0:T(8,128)(2,1)} %gs_hbm.1, bf16[99,16,128]{2,1,0:T(8,128)(2,1)} %rs_hbm.1, ...), custom_call_target="tpu_custom_call" | custom-call | tf_op jit(solution)/shard_map/pallas_call | solution.py:544
  45.8 2.3 %shard_map.150 = (bf16[16,64,512]{2,1,0:T(8,128)(2,1)}, f32[1584,128]{1,0:T(8,128)}) custom-call(bf16[16,64,512]{2,1,0:T(8,128)(2,1)} %get-tuple-element.6.gnext_in, f32[1584,128]{1,0:T(8,128)} %get-tuple-element.7.rnext_in), custom_call_target="tpu_custom_call" | custom-call | tf_op jit(solution)/shard_map/pallas_call | solution.py:561
